TPU v7x, 512 devices: a whole 4x4x16 slice. The times are simulated.
512 devices in a mesh: ctx: 32 (over x, y, core), ch: 16 (over z).
Axes of the slice: x: 4, y: 4, z: 16, core: 2. Of those that a mesh axis runs over, the one named last changes fastest.
Arguments:
- outer_gate: bfloat16 [16, 524288], P(None, ('ctx', 'ch')), may hold values from -6 to 6
- inner_gate: bfloat16 [16, 524288], P(None, ('ctx', 'ch')), may hold values from -6 to 6
- signal: bfloat16 [16, 524288], P(None, ('ctx', 'ch')), may hold values from -6 to 6
- filter_taps: bfloat16 [16, 524288], P(None, ('ctx', 'ch')), may hold values from -1.5 to 1.5
- skip_gain: float32 [16], replicated, may hold values from -3 to 3
Outputs:
- gated: bfloat16 [16, 524288], P(None, ('ctx', 'ch'))
All inputs are finite; a program needn't handle non-finite values.
Results may differ from a plain program's by a relative error of at most 0.012.
Values may be sent and summed in bfloat16 or wider, within the bound.
A program may use at most 64 MiB of HBM per device.

v0:
```python
import math

import jax
import jax.numpy as jnp
from jax import lax
from jax.sharding import PartitionSpec as P


def as_sent(value):

    def short(part):
        return part.astype(jnp.bfloat16) if part.dtype == jnp.float32 else part

    return jax.tree.map(short, value)


def phase_pair(products, period):
    wrapped = products % period
    phase = wrapped.astype(jnp.float32) * (2.0 * math.pi / period)
    return (jnp.cos(phase), jnp.sin(phase))


def grid_phase(row_count, column_count, period):
    row_index = lax.broadcasted_iota(jnp.int32, (row_count, column_count), 0)
    column_index = lax.broadcasted_iota(jnp.int32, (row_count, column_count), 1)
    return phase_pair(row_index * column_index, period)


def pair_frequency(row_index, width):
    half_index = row_index // 2
    mirror = jnp.where(half_index == 0, width // 2, width - half_index)
    return jnp.where(row_index % 2 == 0, half_index, mirror)


def complex_matmul(pattern, matrix_real, matrix_imag, data_real, data_imag):
    exact_mode = lax.Precision.HIGHEST
    real_part = jnp.einsum(pattern, matrix_real, data_real, precision=exact_mode) - jnp.einsum(
        pattern, matrix_imag, data_imag, precision=exact_mode
    )
    imag_part = jnp.einsum(pattern, matrix_real, data_imag, precision=exact_mode) + jnp.einsum(
        pattern, matrix_imag, data_real, precision=exact_mode
    )
    return (real_part, imag_part)


def twiddle(data_real, data_imag, cosine_table, sine_table):
    return (
        data_real * cosine_table - data_imag * sine_table,
        data_real * sine_table + data_imag * cosine_table,
    )


def split_length(length):
    factor = 1
    for candidate in range(1, math.isqrt(length) + 1):
        if length % candidate == 0:
            factor = candidate
    return factor


def local_transform(data_real, data_imag, orient):
    length = data_real.shape[-1]
    inner_size = split_length(length)
    outer_size = length // inner_size
    leading = data_real.shape[:-1]
    shape_two = leading + (outer_size, inner_size)
    cosine_outer, sine_outer = grid_phase(outer_size, outer_size, outer_size)
    part_real, part_imag = complex_matmul(
        "kn,...na->...ka",
        cosine_outer,
        orient * sine_outer,
        data_real.reshape(shape_two),
        data_imag.reshape(shape_two),
    )
    cosine_twist, sine_twist = grid_phase(outer_size, inner_size, length)
    part_real, part_imag = twiddle(part_real, part_imag, cosine_twist, orient * sine_twist)
    cosine_inner, sine_inner = grid_phase(inner_size, inner_size, inner_size)
    part_real, part_imag = complex_matmul(
        "jn,...kn->...jk", cosine_inner, orient * sine_inner, part_real, part_imag
    )
    return (part_real.reshape(leading + (length,)), part_imag.reshape(leading + (length,)))


def complex_times(left_real, left_imag, right_real, right_imag):
    return (
        left_real * right_real - left_imag * right_imag,
        left_real * right_imag + left_imag * right_real,
    )


def local(outer_gate, inner_gate, signal, filter_taps, skip_gain):
    exact_mode = lax.Precision.HIGHEST
    mixed_input = (inner_gate.astype(jnp.float32) * signal.astype(jnp.float32)).astype(jnp.bfloat16)
    grouped_input, grouped_taps = (
        lax.all_to_all(mixed_input, "ch", split_axis=0, concat_axis=1, tiled=True),
        lax.all_to_all(filter_taps, "ch", split_axis=0, concat_axis=1, tiled=True),
    )
    groups, block_cells = grouped_input.shape
    ctx_devices = lax.axis_size("ctx")
    piece_cells = block_cells // ctx_devices
    width = 2 * ctx_devices
    period = width * block_cells
    block_index = lax.axis_index("ctx")
    spread_input, spread_taps = (
        lax.all_to_all(
            grouped_input.reshape(groups, ctx_devices, piece_cells),
            "ctx",
            split_axis=1,
            concat_axis=1,
            tiled=True,
        ),
        lax.all_to_all(
            grouped_taps.reshape(groups, ctx_devices, piece_cells),
            "ctx",
            split_axis=1,
            concat_axis=1,
            tiled=True,
        ),
    )
    row_frequency = pair_frequency(jnp.arange(width, dtype=jnp.int32), width)
    cosine_first, sine_first = phase_pair(
        row_frequency[:, None] * jnp.arange(ctx_devices, dtype=jnp.int32)[None, :], width
    )
    cell_index = block_index * piece_cells + jnp.arange(piece_cells, dtype=jnp.int32)
    cosine_shift, sine_shift = phase_pair(row_frequency[:, None] * cell_index[None, :], period)
    input_values = spread_input.astype(jnp.float32)
    taps_values = spread_taps.astype(jnp.float32)
    input_cos = jnp.einsum("kp,cpq->ckq", cosine_first, input_values, precision=exact_mode)
    input_sin = jnp.einsum("kp,cpq->ckq", sine_first, input_values, precision=exact_mode)
    taps_cos = jnp.einsum("kp,cpq->ckq", cosine_first, taps_values, precision=exact_mode)
    taps_sin = jnp.einsum("kp,cpq->ckq", sine_first, taps_values, precision=exact_mode)
    own_rows = pair_frequency(2 * block_index + jnp.arange(2, dtype=jnp.int32), width)
    cosine_back, sine_back = phase_pair(
        own_rows[:, None] * jnp.arange(block_cells, dtype=jnp.int32)[None, :], period
    )
    inverse_scale = 1.0 / period
    joint_real, joint_imag = twiddle(
        input_cos + taps_sin, taps_cos - input_sin, cosine_shift, -sine_shift
    )
    at_anchor = block_index == 0

    def mirror_of(values):
        flipped = jnp.flip(values, -1)
        anchor_form = jnp.stack([jnp.roll(flipped[:, 0], 1, axis=-1), flipped[:, 1]], axis=1)
        return jnp.where(at_anchor, anchor_form, flipped[:, ::-1])

    piece = lax.all_to_all(
        jnp.stack([joint_real, joint_imag]), "ctx", split_axis=2, concat_axis=3, tiled=True
    )
    mix_real, mix_imag = local_transform(piece[0], piece[1], -1.0)
    mirror_real = mirror_of(mix_real)
    mirror_imag = mirror_of(mix_imag)
    in_real = 0.5 * (mix_real + mirror_real)
    in_imag = 0.5 * (mix_imag - mirror_imag)
    tap_real = 0.5 * (mix_imag + mirror_imag)
    tap_imag = 0.5 * (mirror_real - mix_real)
    prod_real, prod_imag = complex_times(in_real, in_imag, tap_real, tap_imag)
    back_real, back_imag = local_transform(prod_real, prod_imag, 1.0)
    back_real, back_imag = twiddle(back_real, back_imag, cosine_back, sine_back)
    packed_imag = jnp.where(at_anchor, back_real[:, 1], back_imag[:, 0])
    row_groups = back_real.shape[0]
    outgoing = jnp.stack([back_real[:, 0], packed_imag]).reshape(
        2, row_groups, ctx_devices, piece_cells
    )
    returned = lax.all_to_all(
        as_sent(outgoing), "ctx", split_axis=2, concat_axis=2, tiled=True
    ).astype(outgoing.dtype)
    pair_index = jnp.arange(ctx_devices, dtype=jnp.int32)
    fold_cos, fold_sin = phase_pair(pair_index[:, None] * pair_index[None, :], width)
    alternating = 1.0 - 2.0 * (pair_index % 2).astype(jnp.float32)
    weight_cos = jnp.where(pair_index[None, :] == 0, 1.0, 2.0 * fold_cos)
    weight_sin = jnp.where(pair_index[None, :] == 0, -alternating[:, None], 2.0 * fold_sin)
    conv_piece = (
        jnp.einsum("pm,cmq->cpq", weight_cos, returned[0], precision=exact_mode)
        - jnp.einsum("pm,cmq->cpq", weight_sin, returned[1], precision=exact_mode)
    ) * inverse_scale
    conv_piece = conv_piece.astype(jnp.bfloat16)
    conv_rows = lax.all_to_all(conv_piece, "ctx", split_axis=1, concat_axis=1, tiled=True).reshape(
        groups, block_cells
    )
    conv_tokens = lax.all_to_all(conv_rows, "ch", split_axis=1, concat_axis=0, tiled=True)
    total = conv_tokens.astype(jnp.float32) + skip_gain[:, None] * mixed_input.astype(jnp.float32)
    return (outer_gate.astype(jnp.float32) * total).astype(jnp.bfloat16)


def solution(mesh):
    return jax.shard_map(
        local,
        mesh=mesh,
        in_specs=(
            P(None, ("ctx", "ch")),
            P(None, ("ctx", "ch")),
            P(None, ("ctx", "ch")),
            P(None, ("ctx", "ch")),
            P(),
        ),
        out_specs=P(None, ("ctx", "ch")),
        check_vma=False,
    )
```

profile of v0, /device:TPU:1, one launch (start us, length us, event | category | flops | bytes accessed | tf_op | source)
XLA Modules:
  0.0 216.8 jit_solution(11035162921091280176)
XLA Ops:
  2.6 15.7 %all-to-all-start = ((bf16[16,2,512]{2,1,0:T(2,128)(2,1)}), bf16[16,2,512]{2,1,0:T(2,128)(2,1)S(1)}, u32[]{:S(2)}, u32[]{:S(2)}) async-start(bf16[16,2,512]{2,1,0:T(2,128)(2,1)} %reshape.614), calls=%async_computation | async-start | bytes 65536 | tf_op jit(solution)/shard_map/all_to_all | solution.py:95
  18.4 4.5 %fusion.61 = (f32[1,2,16384]{2,0,1:T(1,128)S(1)}, f32[1,2,16384]{2,0,1:T(1,128)S(1)}) fusion(s32[2]{0:T(128)S(1)} %compare_select_fusion.3), kind=kLoop, calls=%fused_computation.111 | loop fusion | flops 458752 | bytes 262152 | tf_op jit(solution)/shard_map/sin | solution.py:20
  24.1 5.7 %all-to-all-done = bf16[16,2,512]{2,1,0:T(2,128)(2,1)S(1)} async-done(((bf16[16,2,512]{2,1,0:T(2,128)(2,1)}), bf16[16,2,512]{2,1,0:T(2,128)(2,1)S(1)}, u32[]{:S(2)}, u32[]{:S(2)}) %all-to-all-start) | async-done | bytes 32800 | tf_op jit(solution)/shard_map/all_to_all | solution.py:95
  29.8 5.8 %all-to-all-start.2 = ((bf16[16,2,512]{2,1,0:T(2,128)(2,1)}), bf16[16,2,512]{2,1,0:T(2,128)(2,1)S(1)}, u32[]{:S(2)}, u32[]{:S(2)}) async-start(bf16[16,2,512]{2,1,0:T(2,128)(2,1)} %reshape.618), calls=%async_computation.2 | async-start | bytes 65536 | tf_op jit(solution)/shard_map/all_to_all | solution.py:96
  37.3 9.7 %all-to-all-done.2 = bf16[16,2,512]{2,1,0:T(2,128)(2,1)S(1)} async-done(((bf16[16,2,512]{2,1,0:T(2,128)(2,1)}), bf16[16,2,512]{2,1,0:T(2,128)(2,1)S(1)}, u32[]{:S(2)}, u32[]{:S(2)}) %all-to-all-start.2) | async-done | bytes 32800 | tf_op jit(solution)/shard_map/all_to_all | solution.py:96
  47.1 9.7 %all-to-all-start.1 = ((bf16[32,2,256]{2,1,0:T(2,128)(2,1)}), bf16[32,2,256]{2,1,0:T(2,128)(2,1)S(1)}, u32[]{:S(2)}, u32[]{:S(2)}) async-start(bf16[32,2,256]{2,1,0:T(2,128)(2,1)} %reshape.616), calls=%async_computation.1 | async-start | bytes 65536 | tf_op jit(solution)/shard_map/all_to_all | solution.py:105
  58.3 5.8 %all-to-all-done.1 = bf16[32,2,256]{2,1,0:T(2,128)(2,1)S(1)} async-done(((bf16[32,2,256]{2,1,0:T(2,128)(2,1)}), bf16[32,2,256]{2,1,0:T(2,128)(2,1)S(1)}, u32[]{:S(2)}, u32[]{:S(2)}) %all-to-all-start.1) | async-done | bytes 32800 | tf_op jit(solution)/shard_map/all_to_all | solution.py:105
  64.1 3.9 %all-to-all-start.3 = ((bf16[32,2,256]{2,1,0:T(2,128)(2,1)}), bf16[32,2,256]{2,1,0:T(2,128)(2,1)S(1)}, u32[]{:S(2)}, u32[]{:S(2)}) async-start(bf16[32,2,256]{2,1,0:T(2,128)(2,1)} %reshape.620), calls=%async_computation.3 | async-start | bytes 65536 | tf_op jit(solution)/shard_map/all_to_all | solution.py:112
  68.8 6.6 %all-to-all-done.3 = bf16[32,2,256]{2,1,0:T(2,128)(2,1)S(1)} async-done(((bf16[32,2,256]{2,1,0:T(2,128)(2,1)}), bf16[32,2,256]{2,1,0:T(2,128)(2,1)S(1)}, u32[]{:S(2)}, u32[]{:S(2)}) %all-to-all-start.3) | async-done | bytes 32800 | tf_op jit(solution)/shard_map/all_to_all | solution.py:112
  76.6 1.0 copy.113
  77.6 3.9 %all-to-all-start.4 = ((f32[2,1,64,512]{3,1,0,2:T(1,128)}), f32[2,1,64,512]{3,1,0,2:T(1,128)S(1)}, u32[]{:S(2)}, u32[]{:S(2)}) async-start(f32[2,1,64,512]{3,1,0,2:T(1,128)} %copy.113), calls=%async_computation.4 | async-start | bytes 524288 | tf_op jit(solution)/shard_map/all_to_all | solution.py:147
  82.3 8.3 %all-to-all-done.4 = f32[2,1,64,512]{3,1,0,2:T(1,128)S(1)} async-done(((f32[2,1,64,512]{3,1,0,2:T(1,128)}), f32[2,1,64,512]{3,1,0,2:T(1,128)S(1)}, u32[]{:S(2)}, u32[]{:S(2)}) %all-to-all-start.4) | async-done | bytes 262176 | tf_op jit(solution)/shard_map/all_to_all | solution.py:147
  95.0 11.5 %rev.10 = f32[1,2,16384]{2,0,1:T(1,128)S(1)} reverse(f32[1,2,16384]{2,0,1:T(1,128)S(1)} %bitcast.189), dimensions={1,2} | reverse | bytes 262144 | tf_op jit(solution)/shard_map/rev | solution.py:145
  107.1 11.5 %rev.9 = f32[1,2,16384]{2,0,1:T(1,128)S(1)} reverse(f32[1,2,16384]{2,0,1:T(1,128)S(1)} %bitcast.192), dimensions={1,2} | reverse | bytes 262144 | tf_op jit(solution)/shard_map/rev | solution.py:145
  118.6 11.1 %slice.71 = f32[1,1,16384]{2,0,1:T(1,128)S(1)} reverse(f32[1,1,16384]{2,0,1:T(1,128)S(1)} %get-tuple-element.13), dimensions={2} | reverse | bytes 131072 | tf_op jit(solution)/shard_map/slice | solution.py:144
  130.4 11.1 %slice.65 = f32[1,1,16384]{2,0,1:T(1,128)S(1)} reverse(f32[1,1,16384]{2,0,1:T(1,128)S(1)} %get-tuple-element.15), dimensions={2} | reverse | bytes 131072 | tf_op jit(solution)/shard_map/slice | solution.py:144
  142.1 11.1 %slice.75 = f32[1,1,16384]{2,0,1:T(1,128)S(1)} reverse(f32[1,1,16384]{2,0,1:T(1,128)S(1)} %get-tuple-element.14), dimensions={2} | reverse | bytes 131072 | tf_op jit(solution)/shard_map/slice | solution.py:144
  153.2 11.1 %slice.69 = f32[1,1,16384]{2,0,1:T(1,128)S(1)} reverse(f32[1,1,16384]{2,0,1:T(1,128)S(1)} %get-tuple-element.16), dimensions={2} | reverse | bytes 131072 | tf_op jit(solution)/shard_map/slice | solution.py:144
  164.3 1.7 maximum_bitcast_fusion
  171.3 4.6 %multiply_subtract_fusion = bf16[1,2,16384]{2,0,1:T(2,128)(2,1)S(1)} fusion(f32[1,2,16384]{2,0,1:T(1,128)S(1)} %bitcast.198, f32[1,2,16384]{2,0,1:T(1,128)S(1)} %bitcast.196, s32[2]{0:T(128)S(1)} %compare_select_fusion.3), kind=kLoop, calls=%fused_computation.56 | loop fusion | flops 589824 | bytes 327688 | tf_op jit(solution)/shard_map/sub | solution.py:48
  177.0 3.7 %all-to-all-start.5 = ((bf16[2,1,32,512]{3,0,1,2:T(2,128)(2,1)}), bf16[2,1,32,512]{3,0,1,2:T(2,128)(2,1)S(1)}, u32[]{:S(2)}, u32[]{:S(2)}) async-start(bf16[2,1,32,512]{3,0,1,2:T(2,128)(2,1)} %pad_maximum_fusion.1), calls=%async_computation.5 | async-start | bytes 131072 | tf_op jit(solution)/shard_map/all_to_all | solution.py:165
  180.7 7.5 %all-to-all-done.5 = bf16[2,1,32,512]{3,0,1,2:T(2,128)(2,1)S(1)} async-done(((bf16[2,1,32,512]{3,0,1,2:T(2,128)(2,1)}), bf16[2,1,32,512]{3,0,1,2:T(2,128)(2,1)S(1)}, u32[]{:S(2)}, u32[]{:S(2)}) %all-to-all-start.5) | async-done | bytes 65568 | tf_op jit(solution)/shard_map/all_to_all | solution.py:165
  189.6 10.8 %all_to_all.74 = bf16[32,2,256]{2,1,0:T(2,128)(2,1)S(1)} all-to-all(bf16[32,2,256]{2,1,0:T(2,128)(2,1)S(1)} %reshape.622), channel_id=1, replica_groups=mesh['ctx'=32,'ch'=16] {'ctx'}, dimensions={0} | all-to-all | bytes 65536 | tf_op jit(solution)/shard_map/all_to_all | solution.py:178
  201.2 14.1 %all_to_all.75 = bf16[16,2,512]{2,1,0:T(2,128)(2,1)S(1)} all-to-all(bf16[16,2,512]{2,1,0:T(2,128)(2,1)S(1)} %reshape.624), channel_id=1, replica_groups=mesh['ctx'=32,'ch'=16] {'ch'}, dimensions={0} | all-to-all | bytes 65536 | tf_op jit(solution)/shard_map/all_to_all | solution.py:181
  (83 shorter events, 26.0 us)
Async XLA Ops:
  2.6 27.2 %all-to-all-start = ((bf16[16,2,512]{2,1,0:T(2,128)(2,1)}), bf16[16,2,512]{2,1,0:T(2,128)(2,1)S(1)}, u32[]{:S(2)}, u32[]{:S(2)}) async-start(bf16[16,2,512]{2,1,0:T(2,128)(2,1)} %reshape.614), calls=%async_computation | async-start | bytes 65536 | tf_op jit(solution)/shard_map/all_to_all | solution.py:95
  18.4 4.5 %copy-start.2 = (bf16[16,1024]{1,0:T(8,128)(2,1)S(1)}, bf16[16,1024]{1,0:T(8,128)(2,1)}, u32[]{:S(2)}) copy-start(bf16[16,1024]{1,0:T(8,128)(2,1)} %param.8) | copy-start | bytes 98308
  29.8 17.3 %all-to-all-start.2 = ((bf16[16,2,512]{2,1,0:T(2,128)(2,1)}), bf16[16,2,512]{2,1,0:T(2,128)(2,1)S(1)}, u32[]{:S(2)}, u32[]{:S(2)}) async-start(bf16[16,2,512]{2,1,0:T(2,128)(2,1)} %reshape.618), calls=%async_computation.2 | async-start | bytes 65536 | tf_op jit(solution)/shard_map/all_to_all | solution.py:96
  47.1 17.0 %all-to-all-start.1 = ((bf16[32,2,256]{2,1,0:T(2,128)(2,1)}), bf16[32,2,256]{2,1,0:T(2,128)(2,1)S(1)}, u32[]{:S(2)}, u32[]{:S(2)}) async-start(bf16[32,2,256]{2,1,0:T(2,128)(2,1)} %reshape.616), calls=%async_computation.1 | async-start | bytes 65536 | tf_op jit(solution)/shard_map/all_to_all | solution.py:105
  64.1 11.3 %all-to-all-start.3 = ((bf16[32,2,256]{2,1,0:T(2,128)(2,1)}), bf16[32,2,256]{2,1,0:T(2,128)(2,1)S(1)}, u32[]{:S(2)}, u32[]{:S(2)}) async-start(bf16[32,2,256]{2,1,0:T(2,128)(2,1)} %reshape.620), calls=%async_computation.3 | async-start | bytes 65536 | tf_op jit(solution)/shard_map/all_to_all | solution.py:112
  77.6 13.0 %all-to-all-start.4 = ((f32[2,1,64,512]{3,1,0,2:T(1,128)}), f32[2,1,64,512]{3,1,0,2:T(1,128)S(1)}, u32[]{:S(2)}, u32[]{:S(2)}) async-start(f32[2,1,64,512]{3,1,0,2:T(1,128)} %copy.113), calls=%async_computation.4 | async-start | bytes 524288 | tf_op jit(solution)/shard_map/all_to_all | solution.py:147
  177.0 11.2 %all-to-all-start.5 = ((bf16[2,1,32,512]{3,0,1,2:T(2,128)(2,1)}), bf16[2,1,32,512]{3,0,1,2:T(2,128)(2,1)S(1)}, u32[]{:S(2)}, u32[]{:S(2)}) async-start(bf16[2,1,32,512]{3,0,1,2:T(2,128)(2,1)} %pad_maximum_fusion.1), calls=%async_computation.5 | async-start | bytes 131072 | tf_op jit(solution)/shard_map/all_to_all | solution.py:165
  215.3 0.8 copy-start
  215.3 0.8 copy-start.1
  215.3 0.8 copy-start.3
  215.3 0.8 copy-start.4
where the time goes:
time: 218 us; the launch traced here: 217 us
  local copies, waits for them, and re-layouts  74.7 us (34%)
  waiting for transfers between devices  43.5 us (20%)
  starting transfers between devices  42.7 us (20%)
  blocking collectives  24.9 us (11%)
  other arithmetic  19.2 us (9%)
  matrix products  11.3 us (5%)
    rev x2, local copies, waits for them, and re-layouts, mirror_of(): return jnp.where(at_anchor, anchor_form, flipped[:, ::-1])  22.9 us
    slice x4, local copies, waits for them, and re-layouts, mirror_of(): flipped[:, 0]  22.3 us
    slice x2, local copies, waits for them, and re-layouts, mirror_of(): flipped[:, 1]  22.2 us
    all_to_all x1, starting transfers between devices, local(): lax.all_to_all(mixed_input, 'ch', split_axis=0, concat_axis=1, tiled=True)  15.7 us
    all_to_all x1, blocking collectives, local(): lax.all_to_all(conv_rows, 'ch', split_axis=1, concat_axis=0, tiled=True)  14.1 us
    all_to_all x1, blocking collectives, local(): lax.all_to_all(conv_piece, 'ctx', split_axis=1, concat_axis=1, tiled=True)  10.8 us
    all_to_all x1, starting transfers between devices, local(): lax.all_to_all(grouped_input.reshape(groups, ctx_devices, piece_cells), '...  9.75 us
    all_to_all x1, waiting for transfers between devices, local(): lax.all_to_all(filter_taps, 'ch', split_axis=0, concat_axis=1, tiled=True)  9.74 us
  transfers between devices with their start and end apart: 6, of which 6 were waited for; matrix products, arithmetic and copies ran while one was open for 5% of the time, Pallas kernels for 0%

commit v1 on v0

v1 whole, which is shorter than its diff:
```python
import functools
import math

import jax
import jax.numpy as jnp
import ml_dtypes
import numpy as np
from jax import lax
from jax.experimental import pallas as pl
from jax.experimental.pallas import tpu as pltpu
from jax.sharding import PartitionSpec as P

MESH = pl.DeviceIdType.MESH
LANES = 128
ROWS = 8


def split_bf16(table):
    high = table.astype(ml_dtypes.bfloat16)
    low = (table - high.astype(np.float64)).astype(ml_dtypes.bfloat16)
    return np.stack([high, low])


def make_tables(planes, blocks):
    units = ROWS * planes
    length = units * LANES
    part = units // blocks
    block, kind, row = np.meshgrid(np.arange(blocks), np.arange(2), np.arange(part), indexing="ij")
    row_first = (block * part + row).reshape(-1)
    row_kind = kind.reshape(-1)
    plane, column_kind, sub = np.meshgrid(np.arange(planes), np.arange(2), np.arange(ROWS), indexing="ij")
    unit = (plane * ROWS + sub).reshape(-1)
    column_kind = column_kind.reshape(-1)
    lane = np.arange(LANES)

    angle = 0.5 * np.pi * LANES * unit[None, :] / length
    angle = angle - 2 * np.pi * ((row_first[:, None] * unit[None, :]) % units) / units
    same = row_kind[:, None] == column_kind[None, :]
    first = np.concatenate([np.cos(angle) * same, np.sin(angle) * same])

    angle = 0.5 * np.pi * lane[None, :] / length - 2 * np.pi * row_first[:, None] * lane[None, :] / length
    twist = np.stack([np.cos(angle), np.sin(angle)])

    angle = 2 * np.pi * ((lane[:, None] * lane[None, :]) % LANES) / LANES
    cosine, sine = np.cos(angle), np.sin(angle)
    second = np.block([[cosine, -sine], [sine, cosine]])
    back = np.concatenate([cosine, sine], axis=1)

    real, imag = twist[0], -twist[1]
    is_real = row_kind[:, None] == 0
    untwist = np.stack([np.where(is_real, real, -imag), np.where(is_real, -imag, -real)])

    every_unit = np.arange(units)
    angle = -0.5 * np.pi * LANES * every_unit[:, None] / length
    angle = angle + 2 * np.pi * ((every_unit[:, None] * row_first[None, :]) % units) / units
    last = np.concatenate([np.cos(angle), -np.sin(angle)], axis=1) / length
    return (
        split_bf16(first),
        twist.astype(np.float32),
        split_bf16(second),
        split_bf16(back),
        untwist.astype(np.float32),
        split_bf16(last),
    )


def dot(left, right):
    return jnp.dot(left, right, preferred_element_type=jnp.float32)


def halves(value):
    high = value.astype(jnp.bfloat16)
    low = (value - high.astype(jnp.float32)).astype(jnp.bfloat16)
    return high, low


def kernel(planes, blocks, inner_hbm, signal_hbm, taps_hbm, outer_hbm, skip_ref, first_hbm, twist_hbm,
           second_hbm, back_hbm, untwist_hbm, last_hbm, out_ref,
           inner, signal, taps, outer, first, twist, second, back, untwist, last,
           mixed, staged, send1, recv1, send2, recv2, xa, xb, ha, hb, send3, recv3, send4, recv4,
           load_sem, send_sem, recv_sem):
    me = lax.axis_index("ctx")
    plane = lax.axis_index("ch")
    channels = planes
    units = ROWS * planes
    part = units // blocks

    barrier = pltpu.get_barrier_semaphore()
    for k in range(1, planes):
        pl.semaphore_signal(barrier, inc=1, device_id=(me, (plane + k) % planes), device_id_type=MESH)
    for k in range(1, blocks):
        pl.semaphore_signal(barrier, inc=1, device_id=((me + k) % blocks, plane), device_id_type=MESH)

    sources = (inner_hbm, signal_hbm, taps_hbm, outer_hbm, first_hbm, twist_hbm, second_hbm, back_hbm,
               untwist_hbm, last_hbm)
    places = (inner, signal, taps, outer, first, twist, second, back, untwist, last)
    loads = [pltpu.make_async_copy(s, d, load_sem.at[i]) for i, (s, d) in enumerate(zip(sources, places))]
    for load in loads:
        load.start()
    for load in loads[:3]:
        load.wait()

    product = inner[...].astype(jnp.float32) * signal[...].astype(jnp.float32)
    product = product.astype(jnp.bfloat16).astype(jnp.float32)
    mixed[...] = product
    filters = taps[...].astype(jnp.float32)
    for s in range(ROWS):
        columns = slice(s * LANES, (s + 1) * LANES)
        staged[pl.ds(s, channels, stride=2 * ROWS), :] = product[:, columns]
        staged[pl.ds(ROWS + s, channels, stride=2 * ROWS), :] = filters[:, columns]
    send1[...] = staged[...].reshape(channels, 2 * ROWS, LANES).astype(jnp.bfloat16)
    recv1[plane] = send1[plane]

    pl.semaphore_wait(barrier, planes + blocks - 2)

    def landing(target, slot):
        if target is recv4:
            return recv4.at[pl.ds(pl.multiple_of(slot * ROWS, ROWS), ROWS)]
        return target.at[slot]

    def exchange(stage, source, target, over_planes):
        size, here = (planes, plane) if over_planes else (blocks, me)
        for k in range(1, size):
            there = (here + k) % size
            pltpu.make_async_remote_copy(
                src_ref=source.at[there],
                dst_ref=landing(target, here),
                send_sem=send_sem.at[stage],
                recv_sem=recv_sem.at[stage],
                device_id=(me, there) if over_planes else (there, plane),
                device_id_type=MESH,
            ).start()

    def whole(stage, source, target):
        size = source.shape[0]
        return pltpu.make_async_remote_copy(
            src_ref=source.at[pl.ds(0, size - 1)],
            dst_ref=target.at[pl.ds(0, (size - 1) * (target.shape[0] // size))],
            send_sem=send_sem.at[stage],
            recv_sem=recv_sem.at[stage],
            device_id=(me, plane),
            device_id_type=MESH,
        )

    exchange(0, send1, recv1, True)
    for load in loads[3:]:
        load.wait()
    whole(0, send1, recv1).wait_recv()

    values = recv1[...].reshape(2 * units, LANES)
    along = dot(first[0], values) + dot(first[1], values)
    real, imag = along[: 2 * units], along[2 * units :]
    turned = jnp.concatenate(
        [real * twist[0] - imag * twist[1], real * twist[1] + imag * twist[0]], axis=1
    )
    high, low = halves(turned)
    spectrum = dot(high, second[0]) + dot(low, second[0]) + dot(high, second[1])
    send2[...] = jnp.concatenate(
        [
            spectrum[:, :LANES].reshape(blocks, ROWS, LANES),
            spectrum[:, LANES:].reshape(blocks, ROWS, LANES),
        ],
        axis=1,
    ).astype(jnp.bfloat16)
    recv2[me] = send2[me]
    exchange(1, send2, recv2, False)
    whole(1, send2, recv2).wait_recv()

    pieces = recv2[...].astype(jnp.float32)
    upper = lax.broadcasted_iota(jnp.int32, (blocks, ROWS, LANES), 1) < part
    real, imag = pieces[:, :ROWS], pieces[:, ROWS:]
    real_rolled = jnp.roll(real, part, axis=1)
    imag_rolled = jnp.roll(imag, part, axis=1)
    xa[...] = jnp.where(upper, real, imag_rolled)
    xb[...] = jnp.where(upper, imag, real_rolled)
    ha[...] = jnp.where(upper, real_rolled, real)
    hb[...] = jnp.where(upper, -imag_rolled, imag)
    sign = jnp.where(lax.broadcasted_iota(jnp.int32, (ROWS, LANES), 0) < part, 1.0, -1.0)
    group = min(8, blocks)
    before = jnp.zeros((ROWS, LANES), jnp.float32)
    for start in range(0, blocks, group):
        sums = [jnp.zeros((ROWS, LANES), jnp.float32) for _ in range(group)]
        for i in range(start + group):
            x_direct, x_crossed = xa[i], xb[i]
            for offset in range(group):
                j = start + offset - i
                if j >= 0:
                    sums[offset] = sums[offset] + (x_direct * ha[j] + x_crossed * hb[j])
        for offset in range(group):
            send3[start + offset] = sums[offset] + sign * jnp.roll(before, part, axis=0)
            before = sums[offset]
    recv3[me] = send3[me]
    exchange(2, send3, recv3, False)
    whole(2, send3, recv3).wait_recv()

    high, low = halves(recv3[...].reshape(2 * units, LANES))
    lanes_back = dot(high, back[0]) + dot(low, back[0]) + dot(high, back[1])
    first_half, second_half = lanes_back[:, :LANES], lanes_back[:, LANES:]
    turned = jnp.concatenate(
        [
            first_half * untwist[0] + second_half * untwist[1],
            second_half * untwist[0] - first_half * untwist[1],
        ],
        axis=0,
    )
    high, low = halves(turned)
    result = dot(last[0], high) + dot(last[0], low) + dot(last[1], high)
    send4[...] = result.reshape(planes, ROWS, LANES)
    landing(recv4, plane)[...] = send4[plane]
    exchange(3, send4, recv4, True)

    channel = lax.broadcasted_iota(jnp.int32, (channels, LANES), 0)
    skip = jnp.zeros((channels, LANES), jnp.float32)
    for c in range(channels):
        skip = jnp.where(channel == c, skip_ref[c], skip)
    whole(3, send4, recv4).wait_recv()

    for s in range(ROWS):
        columns = slice(s * LANES, (s + 1) * LANES)
        conv = recv4[pl.ds(s, channels, stride=ROWS), :].astype(jnp.bfloat16).astype(jnp.float32)
        total = conv + skip * mixed[:, columns]
        out_ref[:, columns] = (outer[:, columns].astype(jnp.float32) * total).astype(jnp.bfloat16)

    whole(0, send1, recv1).wait_send()
    whole(1, send2, recv2).wait_send()
    whole(2, send3, recv3).wait_send()
    whole(3, send4, recv4).wait_send()


def local(planes, blocks, outer_gate, inner_gate, signal, filter_taps, skip_gain):
    channels, tokens = signal.shape
    tables = make_tables(planes, blocks)
    anywhere = pl.BlockSpec(memory_space=pl.ANY)
    bf16, f32 = jnp.bfloat16, jnp.float32
    tile = (ROWS, LANES)
    scratch = [pltpu.VMEM((channels, tokens), bf16)] * 4
    scratch += [pltpu.VMEM(t.shape, t.dtype) for t in tables]
    scratch += [
        pltpu.VMEM((channels, tokens), f32),
        pltpu.VMEM((channels * 2 * ROWS, LANES), f32),
        pltpu.VMEM((channels, 2 * ROWS, LANES), bf16),
        pltpu.VMEM((planes, 2 * ROWS, LANES), bf16),
        pltpu.VMEM((blocks, 2 * ROWS, LANES), bf16),
        pltpu.VMEM((blocks, 2 * ROWS, LANES), bf16),
    ]
    scratch += [pltpu.VMEM((blocks,) + tile, f32)] * 6
    scratch += [pltpu.VMEM((planes,) + tile, f32)]
    scratch += [pltpu.VMEM((planes * ROWS, LANES), f32)]
    scratch += [
        pltpu.SemaphoreType.DMA((10,)),
        pltpu.SemaphoreType.DMA((4,)),
        pltpu.SemaphoreType.DMA((4,)),
    ]
    return pl.pallas_call(
        functools.partial(kernel, planes, blocks),
        out_shape=jax.ShapeDtypeStruct((channels, tokens), bf16),
        in_specs=[anywhere] * 4 + [pl.BlockSpec(memory_space=pltpu.SMEM)] + [anywhere] * 6,
        out_specs=pl.BlockSpec(memory_space=pltpu.VMEM),
        scratch_shapes=scratch,
        compiler_params=pltpu.CompilerParams(collective_id=0, has_side_effects=True),
        name="hyena_conv",
    )(inner_gate, signal, filter_taps, outer_gate, skip_gain, *[jnp.asarray(t) for t in tables])


def solution(mesh):
    spec = P(None, ("ctx", "ch"))
    return jax.shard_map(
        functools.partial(local, mesh.shape["ch"], mesh.shape["ctx"]),
        mesh=mesh,
        in_specs=(spec, spec, spec, spec, P()),
        out_specs=spec,
        check_vma=False,
    )
```

time: 218 us -> 49.1 us (0.23)
  local copies, waits for them, and re-layouts: 74.7 us -> 1.38 us
  Pallas kernels: 0 us -> 47.5 us
  waiting for transfers between devices: 43.5 us -> 0 us
  starting transfers between devices: 42.7 us -> 0 us
  blocking collectives: 24.9 us -> 0 us
  other arithmetic: 19.2 us -> 0 us
  matrix products: 11.3 us -> 0 us
    pallas_call x0 -> x1, Pallas kernels: none -> 47.5 us  [local(): pl.pallas_call(functools.partial(kernel, planes, blocks), out_shape=jax.S...]
    slice x10 -> x0, local copies, waits for them, and re-layouts: 45.9 us -> none  [the longest x4 22.3 us: mirror_of(): flipped[:, 0]]
    all_to_all x6 -> x0, waiting for transfers between devices: 43.5 us -> none  [the longest x1 9.74 us: local(): lax.all_to_all(filter_taps, 'ch', split_axis=0, concat_axis=1, tiled=True)]
    all_to_all x6 -> x0, starting transfers between devices: 42.7 us -> none  [the longest x1 15.7 us: local(): lax.all_to_all(mixed_input, 'ch', split_axis=0, concat_axis=1, tiled=True)]
    all_to_all x2 -> x0, blocking collectives: 24.9 us -> none  [the longest x1 14.1 us: local(): lax.all_to_all(conv_rows, 'ch', split_axis=1, concat_axis=0, tiled=True)]
    rev x2 -> x0, local copies, waits for them, and re-layouts: 22.9 us -> none  [mirror_of(): return jnp.where(at_anchor, anchor_form, flipped[:, ::-1])]
    dot_general x22 -> x0, matrix products: 11.3 us -> none  [the longest x4 2.24 us: complex_matmul(): jnp.einsum(pattern, matrix_imag, data_imag, precision=exact_mode)]
    sub x2 -> x0, other arithmetic: 5.24 us -> none  [the longest x1 4.63 us: twiddle(): data_real * cosine_table - data_imag * sine_table]
  transfers between devices with their start and end apart: 6 -> 0, of which waited for: 6 -> 0; matrix products, arithmetic and copies ran while one was open for 5% -> 0% of each run, Pallas kernels for 0% -> 0%
where the time goes in v1:
time: 49.1 us; the launch traced here: 48.9 us
  Pallas kernels  47.5 us (97%)
  local copies, waits for them, and re-layouts  1.38 us (3%)
    pallas_call x1, Pallas kernels, local(): pl.pallas_call(functools.partial(kernel, planes, blocks), out_shape=jax.S...  47.5 us
    unnamed x1, local copies, waits for them, and re-layouts  1.38 us

profile of v1, /device:TPU:1, one launch (start us, length us, event | category | flops | bytes accessed | tf_op | source)
XLA Modules:
  0.0 48.9 jit_solution(11561469855064689446)
XLA Ops:
  0.0 47.5 %hyena_conv.1 = bf16[16,1024]{1,0:T(8,128)(2,1)} custom-call(bf16[16,1024]{1,0:T(8,128)(2,1)} %inner_hbm.1, bf16[16,1024]{1,0:T(8,128)(2,1)} %signal_hbm.1, bf16[16,1024]{1,0:T(8,128)(2,1)} %taps_hbm.1, bf16[16,1024]{1,0:T(8,128)(2,1)} %outer_hbm.1, f32[16]{0:T(128)} %skip_ref.1, bf16[2,512,256]{2,1,0:T(8,128)(2,1)} %constant.12.clone.first_hbm, ...), custom_call_target="tpu_custom_call" | custom-call | tf_op jit(solution)/shard_map/hyena_conv/pallas_call | solution.py:254
  47.5 1.4 %copy.13 = bf16[16,1024]{1,0:T(8,128)(2,1)} copy(bf16[16,1024]{1,0:T(8,128)(2,1)} %hyena_conv.1) | data formatting | bytes 65536

commit v2 on v1

--- a/solution.py
+++ b/solution.py
@@ -74,6 +74,19 @@
     return high, low
 
 
+def far_first(size, ring):
+    def around(k, n):
+        return min(k, n - k)
+
+    def distance(k):
+        if ring:
+            return around(k, size)
+        side = max(1, math.isqrt(size // 2))
+        return around(k // (2 * side), side) + around(k // 2 % side, side)
+
+    return sorted(range(1, size), key=lambda k: -distance(k))
+
+
 def kernel(planes, blocks, inner_hbm, signal_hbm, taps_hbm, outer_hbm, skip_ref, first_hbm, twist_hbm,
            second_hbm, back_hbm, untwist_hbm, last_hbm, out_ref,
            inner, signal, taps, outer, first, twist, second, back, untwist, last,
@@ -120,7 +133,7 @@
 
     def exchange(stage, source, target, over_planes):
         size, here = (planes, plane) if over_planes else (blocks, me)
-        for k in range(1, size):
+        for k in far_first(size, over_planes):
             there = (here + k) % size
             pltpu.make_async_remote_copy(
                 src_ref=source.at[there],

time: 49.1 us -> 45.3 us (0.923)
  Pallas kernels: 47.5 us -> 43.7 us
    pallas_call x1, Pallas kernels: 47.5 us -> 43.7 us  [local(): pl.pallas_call(functools.partial(kernel, planes, blocks), out_shape=jax.S...]
where the time goes in v2:
time: 45.3 us; the launch traced here: 45.1 us
  Pallas kernels  43.7 us (96%)
  local copies, waits for them, and re-layouts  1.38 us (3%)
    pallas_call x1, Pallas kernels, local(): pl.pallas_call(functools.partial(kernel, planes, blocks), out_shape=jax.S...  43.7 us
    unnamed x1, local copies, waits for them, and re-layouts  1.38 us

profile of v2, /device:TPU:1, one launch (start us, length us, event | category | flops | bytes accessed | tf_op | source)
XLA Modules:
  0.0 45.1 jit_solution(14570816783814828243)
XLA Ops:
  0.0 43.7 %hyena_conv.1 = bf16[16,1024]{1,0:T(8,128)(2,1)} custom-call(bf16[16,1024]{1,0:T(8,128)(2,1)} %inner_hbm.1, bf16[16,1024]{1,0:T(8,128)(2,1)} %signal_hbm.1, bf16[16,1024]{1,0:T(8,128)(2,1)} %taps_hbm.1, bf16[16,1024]{1,0:T(8,128)(2,1)} %outer_hbm.1, f32[16]{0:T(128)} %skip_ref.1, bf16[2,512,256]{2,1,0:T(8,128)(2,1)} %constant.12.clone.first_hbm, ...), custom_call_target="tpu_custom_call" | custom-call | tf_op jit(solution)/shard_map/hyena_conv/pallas_call | solution.py:267
  43.7 1.4 %copy.13 = bf16[16,1024]{1,0:T(8,128)(2,1)} copy(bf16[16,1024]{1,0:T(8,128)(2,1)} %hyena_conv.1) | data formatting | bytes 65536

commit v3 on v2

v3 whole, which is shorter than its diff:
```python
import functools
import math

import jax
import jax.numpy as jnp
import ml_dtypes
import numpy as np
from jax import lax
from jax.experimental import pallas as pl
from jax.experimental.pallas import tpu as pltpu
from jax.sharding import PartitionSpec as P

MESH = pl.DeviceIdType.MESH
LANES = 128
ROWS = 8
PAIR = 2
SHIFT = 1


def split_bf16(table):
    high = table.astype(ml_dtypes.bfloat16)
    low = (table - high.astype(np.float64)).astype(ml_dtypes.bfloat16)
    return np.stack([high, low])


def make_tables(planes, blocks):
    units = ROWS * planes
    length = units * LANES
    part = units // blocks
    block, kind, row = np.meshgrid(np.arange(blocks), np.arange(2), np.arange(part), indexing="ij")
    row_first = (block * part + row).reshape(-1)
    row_kind = kind.reshape(-1)
    plane, column_kind, sub = np.meshgrid(np.arange(planes), np.arange(2), np.arange(ROWS), indexing="ij")
    unit = (plane * ROWS + sub).reshape(-1)
    column_kind = column_kind.reshape(-1)
    lane = np.arange(LANES)

    angle = 0.5 * np.pi * LANES * unit[None, :] / length
    angle = angle - 2 * np.pi * ((row_first[:, None] * unit[None, :]) % units) / units
    same = row_kind[:, None] == column_kind[None, :]
    first = np.concatenate([np.cos(angle) * same, np.sin(angle) * same])

    angle = 0.5 * np.pi * lane[None, :] / length - 2 * np.pi * row_first[:, None] * lane[None, :] / length
    twist = np.stack([np.cos(angle), np.sin(angle)])

    angle = 2 * np.pi * ((lane[:, None] * lane[None, :]) % LANES) / LANES
    cosine, sine = np.cos(angle), np.sin(angle)
    second = np.block([[cosine, -sine], [sine, cosine]])
    back = np.concatenate([cosine, sine], axis=1)

    real, imag = twist[0], -twist[1]
    is_real = row_kind[:, None] == 0
    untwist = np.stack([np.where(is_real, real, -imag), np.where(is_real, -imag, -real)])

    every_unit = np.arange(units)
    angle = -0.5 * np.pi * LANES * every_unit[:, None] / length
    angle = angle + 2 * np.pi * ((every_unit[:, None] * row_first[None, :]) % units) / units
    last = np.concatenate([np.cos(angle), -np.sin(angle)], axis=1) / length
    return (
        split_bf16(first),
        twist.astype(np.float32),
        split_bf16(second),
        split_bf16(back),
        untwist.astype(np.float32),
        split_bf16(last),
    )


def dot(left, right):
    return jnp.dot(left, right, preferred_element_type=jnp.float32)


def halves(value):
    high = value.astype(jnp.bfloat16)
    low = (value - high.astype(jnp.float32)).astype(jnp.bfloat16)
    return high, low


def far_first(size, ring):
    def around(k, n):
        return min(k, n - k)

    def distance(k):
        if ring:
            return around(k, size)
        side = max(1, math.isqrt(size // 2))
        return around(k // (2 * side), side) + around(k // 2 % side, side)

    return sorted(range(1, size), key=lambda k: -distance(k))


def kernel(planes, blocks, inner_hbm, signal_hbm, taps_hbm, outer_hbm, skip_hbm, first_hbm, twist_hbm,
           second_hbm, back_hbm, untwist_hbm, last_hbm, out_ref,
           inner, signal, taps, outer, skip_scalars, first, twist, second, back, untwist, last,
           mixed, staged, send1, recv1, send2, recv2, xa, xb, ha, hb, product, send3, recv3, send4, recv4, rows4,
           load_sem, send_sem, recv_sem):
    me = lax.axis_index("ctx")
    plane = lax.axis_index("ch")
    channels = planes
    owners = planes // PAIR

    def rank(z):
        return (z + SHIFT) % planes

    units = ROWS * planes
    part = units // blocks
    is_owner = rank(plane) < owners
    mine = rank(plane)
    ring = far_first(planes, True)
    flat = far_first(blocks, False)

    barrier = pltpu.get_barrier_semaphore()

    @pl.when(is_owner)
    def _():
        for k in ring:
            pl.semaphore_signal(barrier, inc=1, device_id=(me, (plane + k) % planes), device_id_type=MESH)
        for k in flat:
            pl.semaphore_signal(barrier, inc=1, device_id=((me + k) % blocks, plane), device_id_type=MESH)

    sources = (inner_hbm, signal_hbm, taps_hbm, outer_hbm, skip_hbm, first_hbm, twist_hbm, second_hbm,
               back_hbm, untwist_hbm, last_hbm)
    places = (inner, signal, taps, outer, skip_scalars, first, twist, second, back, untwist, last)
    loads = [pltpu.make_async_copy(s, d, load_sem.at[i]) for i, (s, d) in enumerate(zip(sources, places))]
    for load in loads[:5]:
        load.start()
    for load in loads[:3]:
        load.wait()

    gated = inner[...].astype(jnp.float32) * signal[...].astype(jnp.float32)
    gated = gated.astype(jnp.bfloat16).astype(jnp.float32)
    mixed[...] = gated
    filters = taps[...].astype(jnp.float32)
    for s in range(ROWS):
        columns = slice(s * LANES, (s + 1) * LANES)
        staged[pl.ds(s, channels, stride=2 * ROWS), :] = gated[:, columns]
        staged[pl.ds(ROWS + s, channels, stride=2 * ROWS), :] = filters[:, columns]
    send1[...] = staged[...].reshape(owners, PAIR * 2 * ROWS, LANES).astype(jnp.bfloat16)

    pl.semaphore_wait(barrier, jnp.where(is_owner, owners + blocks - 2, owners))

    def remote(stage, source, target, device):
        return pltpu.make_async_remote_copy(
            src_ref=source,
            dst_ref=target,
            send_sem=send_sem.at[stage],
            recv_sem=recv_sem.at[stage],
            device_id=device,
            device_id_type=MESH,
        )

    def whole(stage, buffer, slots):
        return remote(stage, buffer.at[pl.ds(0, slots)], buffer.at[pl.ds(0, slots)], (me, plane))

    for k in ring:
        there = (plane + k) % planes

        @pl.when(rank(there) < owners)
        def _(there=there):
            remote(0, send1.at[rank(there)], recv1.at[plane], (me, there)).start()

    @pl.when(is_owner)
    def _():
        for load in loads[5:]:
            load.start()
        recv1[plane] = send1[mine]
        for load in loads[5:]:
            load.wait()
        whole(0, recv1, planes - 1).wait_recv()

        per_channel = 2 * ROWS
        values = jnp.concatenate(
            [
                recv1[:, c * per_channel : (c + 1) * per_channel, :].reshape(2 * units, LANES)
                for c in range(PAIR)
            ],
            axis=1,
        )
        along = dot(first[0], values) + dot(first[1], values)
        for c in range(PAIR):
            real = along[: 2 * units, c * LANES : (c + 1) * LANES]
            imag = along[2 * units :, c * LANES : (c + 1) * LANES]
            turned = jnp.concatenate(
                [real * twist[0] - imag * twist[1], real * twist[1] + imag * twist[0]], axis=1
            )
            high, low = halves(turned)
            spectrum = dot(high, second[0]) + dot(low, second[0]) + dot(high, second[1])
            send2[c] = jnp.concatenate(
                [
                    spectrum[:, :LANES].reshape(blocks, ROWS, LANES),
                    spectrum[:, LANES:].reshape(blocks, ROWS, LANES),
                ],
                axis=1,
            ).astype(jnp.bfloat16)
            recv2[c, me] = send2[c, me]
            for k in flat:
                there = (me + k) % blocks
                remote(1 + c, send2.at[c, there], recv2.at[c, me], (there, plane)).start()

        upper = lax.broadcasted_iota(jnp.int32, (blocks, ROWS, LANES), 1) < part
        sign = jnp.where(lax.broadcasted_iota(jnp.int32, (ROWS, LANES), 0) < part, 1.0, -1.0)
        group = min(8, blocks)
        for c in range(PAIR):
            whole(1 + c, recv2.at[c], blocks - 1).wait_recv()
            pieces = recv2[c].astype(jnp.float32)
            real, imag = pieces[:, :ROWS], pieces[:, ROWS:]
            real_rolled = jnp.roll(real, part, axis=1)
            imag_rolled = jnp.roll(imag, part, axis=1)
            xa[...] = jnp.where(upper, real, imag_rolled)
            xb[...] = jnp.where(upper, imag, real_rolled)
            ha[...] = jnp.where(upper, real_rolled, real)
            hb[...] = jnp.where(upper, -imag_rolled, imag)
            before = jnp.zeros((ROWS, LANES), jnp.float32)
            for start in range(0, blocks, group):
                sums = [jnp.zeros((ROWS, LANES), jnp.float32) for _ in range(group)]
                for i in range(start + group):
                    x_direct, x_crossed = xa[i], xb[i]
                    for offset in range(group):
                        j = start + offset - i
                        if j >= 0:
                            sums[offset] = sums[offset] + (x_direct * ha[j] + x_crossed * hb[j])
                for offset in range(group):
                    product[start + offset, c * ROWS : (c + 1) * ROWS, :] = sums[offset] + sign * jnp.roll(
                        before, part, axis=0
                    )
                    before = sums[offset]
        send3[...] = product[...].astype(jnp.bfloat16)
        recv3[me] = send3[me]
        for k in flat:
            there = (me + k) % blocks
            remote(1 + PAIR, send3.at[there], recv3.at[me], (there, plane)).start()
        whole(1 + PAIR, recv3, blocks - 1).wait_recv()

        waves = recv3[...].reshape(blocks * PAIR * ROWS, LANES)
        lanes_back = (dot(waves, back[0]) + dot(waves, back[1])).reshape(blocks, PAIR, ROWS, 2 * LANES)
        turned = []
        for c in range(PAIR):
            lanes_c = lanes_back[:, c].reshape(2 * units, 2 * LANES)
            first_half, second_half = lanes_c[:, :LANES], lanes_c[:, LANES:]
            turned.append(
                jnp.concatenate(
                    [
                        first_half * untwist[0] + second_half * untwist[1],
                        second_half * untwist[0] - first_half * untwist[1],
                    ],
                    axis=0,
                )
            )
        high, low = halves(jnp.concatenate(turned, axis=1))
        result = dot(last[0], high) + dot(last[0], low) + dot(last[1], high)
        send4[...] = jnp.concatenate(
            [result[:, c * LANES : (c + 1) * LANES].reshape(planes, ROWS, LANES) for c in range(PAIR)], axis=1
        ).astype(jnp.bfloat16)
        recv4[mine] = send4[plane]
        for k in ring:
            there = (plane + k) % planes
            remote(2 + PAIR, send4.at[there], recv4.at[mine], (me, there)).start()

    channel = lax.broadcasted_iota(jnp.int32, (channels, LANES), 0)
    loads[3].wait()
    loads[4].wait()
    skip = jnp.zeros((channels, LANES), jnp.float32)
    for c in range(channels):
        skip = jnp.where(channel == c, skip_scalars[c], skip)

    @pl.when(is_owner)
    def _():
        whole(2 + PAIR, recv4, owners - 1).wait_recv()

    @pl.when(jnp.logical_not(is_owner))
    def _():
        whole(2 + PAIR, recv4, owners).wait_recv()

    rows4[...] = recv4[...].astype(jnp.float32).reshape(channels * ROWS, LANES)
    for s in range(ROWS):
        columns = slice(s * LANES, (s + 1) * LANES)
        conv = rows4[pl.ds(s, channels, stride=ROWS), :]
        total = conv + skip * mixed[:, columns]
        out_ref[:, columns] = (outer[:, columns].astype(jnp.float32) * total).astype(jnp.bfloat16)

    @pl.when(is_owner)
    def _():
        whole(0, send1, owners - 1).wait_send()
        for c in range(PAIR):
            whole(1 + c, send2.at[c], blocks - 1).wait_send()
        whole(1 + PAIR, send3, blocks - 1).wait_send()
        whole(2 + PAIR, send4, planes - 1).wait_send()

    @pl.when(jnp.logical_not(is_owner))
    def _():
        whole(0, send1, owners).wait_send()


def local(planes, blocks, outer_gate, inner_gate, signal, filter_taps, skip_gain):
    channels, tokens = signal.shape
    owners = planes // PAIR
    tables = make_tables(planes, blocks)
    bf16, f32 = jnp.bfloat16, jnp.float32
    scratch = [pltpu.VMEM((channels, tokens), bf16)] * 4
    scratch += [pltpu.SMEM((channels,), f32)]
    scratch += [pltpu.VMEM(t.shape, t.dtype) for t in tables]
    scratch += [
        pltpu.VMEM((channels, tokens), f32),
        pltpu.VMEM((channels * 2 * ROWS, LANES), f32),
        pltpu.VMEM((owners, PAIR * 2 * ROWS, LANES), bf16),
        pltpu.VMEM((planes, PAIR * 2 * ROWS, LANES), bf16),
        pltpu.VMEM((PAIR, blocks, 2 * ROWS, LANES), bf16),
        pltpu.VMEM((PAIR, blocks, 2 * ROWS, LANES), bf16),
    ]
    scratch += [pltpu.VMEM((blocks, ROWS, LANES), f32)] * 4
    scratch += [
        pltpu.VMEM((blocks, PAIR * ROWS, LANES), f32),
        pltpu.VMEM((blocks, PAIR * ROWS, LANES), bf16),
        pltpu.VMEM((blocks, PAIR * ROWS, LANES), bf16),
        pltpu.VMEM((planes, PAIR * ROWS, LANES), bf16),
        pltpu.VMEM((owners, PAIR * ROWS, LANES), bf16),
        pltpu.VMEM((channels * ROWS, LANES), f32),
        pltpu.SemaphoreType.DMA((11,)),
        pltpu.SemaphoreType.DMA((3 + PAIR,)),
        pltpu.SemaphoreType.DMA((3 + PAIR,)),
    ]
    operands = (inner_gate, signal, filter_taps, outer_gate, skip_gain, *[jnp.asarray(t) for t in tables])
    return pl.pallas_call(
        functools.partial(kernel, planes, blocks),
        out_shape=pltpu.VMEM((channels, tokens), bf16),
        in_specs=[pl.BlockSpec(memory_space=pltpu.HBM)] * len(operands),
        out_specs=pl.BlockSpec(memory_space=pltpu.VMEM),
        scratch_shapes=scratch,
        compiler_params=pltpu.CompilerParams(
            collective_id=0, has_side_effects=True, vmem_limit_bytes=16 * 2**20
        ),
        name="hyena_conv",
    )(*[pltpu.with_memory_space_constraint(operand, pltpu.HBM) for operand in operands])


def solution(mesh):
    spec = P(None, ("ctx", "ch"))
    return jax.shard_map(
        functools.partial(local, mesh.shape["ch"], mesh.shape["ctx"]),
        mesh=mesh,
        in_specs=(spec, spec, spec, spec, P()),
        out_specs=spec,
        check_vma=False,
    )
```

time: 45.3 us -> 43 us (0.949)
  Pallas kernels: 43.7 us -> 42.2 us
  local copies, waits for them, and re-layouts: 1.38 us -> 0.62 us
    pallas_call x1, Pallas kernels: 43.7 us -> 42.2 us  [local(): pl.pallas_call(functools.partial(kernel, planes, blocks), out_shape=pltpu...]
    unnamed x1, local copies, waits for them, and re-layouts: 1.38 us -> 0.62 us
where the time goes in v3:
time: 43 us; the launch traced here: 42.8 us
  Pallas kernels  42.2 us (98%)
  local copies, waits for them, and re-layouts  0.62 us (1%)
    pallas_call x1, Pallas kernels, local(): pl.pallas_call(functools.partial(kernel, planes, blocks), out_shape=pltpu...  42.2 us

profile of v3, /device:TPU:1, one launch (start us, length us, event | category | flops | bytes accessed | tf_op | source)
XLA Modules:
  0.0 42.8 jit_solution(16842776554663684734)
XLA Ops:
  0.0 42.2 %hyena_conv.1 = bf16[16,1024]{1,0:T(8,128)(2,1)S(1)} custom-call(bf16[16,1024]{1,0:T(8,128)(2,1)} %inner_hbm.1, bf16[16,1024]{1,0:T(8,128)(2,1)} %signal_hbm.1, bf16[16,1024]{1,0:T(8,128)(2,1)} %taps_hbm.1, bf16[16,1024]{1,0:T(8,128)(2,1)} %outer_hbm.1, f32[16]{0:T(128)} %skip_hbm.1, bf16[2,512,256]{2,1,0:T(8,128)(2,1)} %constant.12.clone.first_hbm, ...), custom_call_target="tpu_custom_call" | custom-call | tf_op jit(solution)/shard_map/hyena_conv/pallas_call | solution.py:323
  42.2 0.6 %copy.13 = bf16[16,1024]{1,0:T(8,128)(2,1)} copy(bf16[16,1024]{1,0:T(8,128)(2,1)S(1)} %hyena_conv.1) | data formatting | bytes 65536

commit v4 on v3

--- a/solution.py
+++ b/solution.py
@@ -14,7 +14,7 @@
 LANES = 128
 ROWS = 8
 PAIR = 2
-SHIFT = 1
+DOUBLES_IN_EIGHT = 3
 
 
 def split_bf16(table):
@@ -60,9 +60,9 @@
         split_bf16(first),
         twist.astype(np.float32),
         split_bf16(second),
-        split_bf16(back),
+        back.astype(ml_dtypes.bfloat16),
         untwist.astype(np.float32),
-        split_bf16(last),
+        last.astype(ml_dtypes.bfloat16),
     )
 
 
@@ -76,17 +76,23 @@
     return high, low
 
 
-def far_first(size, ring):
+def away(k, size, ring):
     def around(k, n):
         return min(k, n - k)
 
-    def distance(k):
-        if ring:
-            return around(k, size)
-        side = max(1, math.isqrt(size // 2))
-        return around(k // (2 * side), side) + around(k // 2 % side, side)
-
-    return sorted(range(1, size), key=lambda k: -distance(k))
+    if ring:
+        return around(k, size)
+    side = max(1, math.isqrt(size // 2))
+    return around(k // (2 * side), side) + around(k // 2 % side, side)
+
+
+def far_first(size, ring):
+    return sorted(range(1, size), key=lambda k: -away(k, size, ring))
+
+
+def layout(planes):
+    doubles = DOUBLES_IN_EIGHT * planes // 8
+    return planes - PAIR * doubles, doubles
 
 
 def kernel(planes, blocks, inner_hbm, signal_hbm, taps_hbm, outer_hbm, skip_hbm, first_hbm, twist_hbm,
@@ -97,15 +103,18 @@
     me = lax.axis_index("ctx")
     plane = lax.axis_index("ch")
     channels = planes
-    owners = planes // PAIR
+    singles, doubles = layout(planes)
+    owners = singles + doubles
 
     def rank(z):
-        return (z + SHIFT) % planes
+        return (z + singles) % planes
 
     units = ROWS * planes
     part = units // blocks
     is_owner = rank(plane) < owners
     mine = rank(plane)
+    is_double = jnp.logical_and(mine >= singles, mine < owners)
+    is_single = mine < singles
     ring = far_first(planes, True)
     flat = far_first(blocks, False)
 
@@ -135,7 +144,7 @@
         columns = slice(s * LANES, (s + 1) * LANES)
         staged[pl.ds(s, channels, stride=2 * ROWS), :] = gated[:, columns]
         staged[pl.ds(ROWS + s, channels, stride=2 * ROWS), :] = filters[:, columns]
-    send1[...] = staged[...].reshape(owners, PAIR * 2 * ROWS, LANES).astype(jnp.bfloat16)
+    send1[...] = staged[...].reshape(channels, 2 * ROWS, LANES).astype(jnp.bfloat16)
 
     pl.semaphore_wait(barrier, jnp.where(is_owner, owners + blocks - 2, owners))
 
@@ -149,35 +158,50 @@
             device_id_type=MESH,
         )
 
+    def channel_of(owner):
+        return singles + PAIR * (owner - singles)
+
     def whole(stage, buffer, slots):
         return remote(stage, buffer.at[pl.ds(0, slots)], buffer.at[pl.ds(0, slots)], (me, plane))
 
     for k in ring:
         there = (plane + k) % planes
 
-        @pl.when(rank(there) < owners)
+        @pl.when(rank(there) < singles)
         def _(there=there):
-            remote(0, send1.at[rank(there)], recv1.at[plane], (me, there)).start()
+            remote(0, send1.at[rank(there)], recv1.at[plane, 0], (me, there)).start()
+
+        @pl.when(jnp.logical_and(rank(there) >= singles, rank(there) < owners))
+        def _(there=there):
+            remote(0, send1.at[pl.ds(channel_of(rank(there)), PAIR)], recv1.at[plane], (me, there)).start()
 
     @pl.when(is_owner)
     def _():
         for load in loads[5:]:
             load.start()
-        recv1[plane] = send1[mine]
+
+        @pl.when(is_single)
+        def _():
+            recv1[plane, 0] = send1[mine]
+
+        @pl.when(is_double)
+        def _():
+            recv1[plane] = send1[pl.ds(channel_of(mine), PAIR)]
+
         for load in loads[5:]:
             load.wait()
-        whole(0, recv1, planes - 1).wait_recv()
-
-        per_channel = 2 * ROWS
-        values = jnp.concatenate(
-            [
-                recv1[:, c * per_channel : (c + 1) * per_channel, :].reshape(2 * units, LANES)
-                for c in range(PAIR)
-            ],
-            axis=1,
-        )
+
+        @pl.when(is_single)
+        def _():
+            whole(0, recv1.at[:, 0], planes - 1).wait_recv()
+
+        @pl.when(is_double)
+        def _():
+            whole(0, recv1, planes - 1).wait_recv()
+
+        values = jnp.concatenate([recv1[:, c].reshape(2 * units, LANES) for c in range(PAIR)], axis=1)
         along = dot(first[0], values) + dot(first[1], values)
-        for c in range(PAIR):
+        def forward(c):
             real = along[: 2 * units, c * LANES : (c + 1) * LANES]
             imag = along[2 * units :, c * LANES : (c + 1) * LANES]
             turned = jnp.concatenate(
@@ -197,10 +221,13 @@
                 there = (me + k) % blocks
                 remote(1 + c, send2.at[c, there], recv2.at[c, me], (there, plane)).start()
 
+        forward(0)
+        pl.when(is_double)(functools.partial(forward, 1))
+
         upper = lax.broadcasted_iota(jnp.int32, (blocks, ROWS, LANES), 1) < part
         sign = jnp.where(lax.broadcasted_iota(jnp.int32, (ROWS, LANES), 0) < part, 1.0, -1.0)
         group = min(8, blocks)
-        for c in range(PAIR):
+        def multiply(c):
             whole(1 + c, recv2.at[c], blocks - 1).wait_recv()
             pieces = recv2[c].astype(jnp.float32)
             real, imag = pieces[:, :ROWS], pieces[:, ROWS:]
@@ -224,15 +251,25 @@
                         before, part, axis=0
                     )
                     before = sums[offset]
+
+        multiply(0)
+        pl.when(is_double)(functools.partial(multiply, 1))
+
+        @pl.when(is_single)
+        def _():
+            product[:, ROWS:, :] = jnp.zeros((blocks, ROWS, LANES), jnp.float32)
+
         send3[...] = product[...].astype(jnp.bfloat16)
         recv3[me] = send3[me]
-        for k in flat:
-            there = (me + k) % blocks
-            remote(1 + PAIR, send3.at[there], recv3.at[me], (there, plane)).start()
+        for there in sorted(range(blocks), key=lambda k: away(k, blocks, False)):
+
+            @pl.when(there != me)
+            def _(there=there):
+                remote(1 + PAIR, send3.at[there], recv3.at[me], (there, plane)).start()
         whole(1 + PAIR, recv3, blocks - 1).wait_recv()
 
         waves = recv3[...].reshape(blocks * PAIR * ROWS, LANES)
-        lanes_back = (dot(waves, back[0]) + dot(waves, back[1])).reshape(blocks, PAIR, ROWS, 2 * LANES)
+        lanes_back = dot(waves, back[...]).reshape(blocks, PAIR, ROWS, 2 * LANES)
         turned = []
         for c in range(PAIR):
             lanes_c = lanes_back[:, c].reshape(2 * units, 2 * LANES)
@@ -246,15 +283,21 @@
                     axis=0,
                 )
             )
-        high, low = halves(jnp.concatenate(turned, axis=1))
-        result = dot(last[0], high) + dot(last[0], low) + dot(last[1], high)
+        result = dot(last[...], jnp.concatenate(turned, axis=1).astype(jnp.bfloat16))
         send4[...] = jnp.concatenate(
             [result[:, c * LANES : (c + 1) * LANES].reshape(planes, ROWS, LANES) for c in range(PAIR)], axis=1
         ).astype(jnp.bfloat16)
         recv4[mine] = send4[plane]
         for k in ring:
             there = (plane + k) % planes
+            if 1: continue
             remote(2 + PAIR, send4.at[there], recv4.at[mine], (me, there)).start()
+
+        for there in range(planes):
+
+            @pl.when(there != plane)
+            def _(there=there):
+                remote(2 + PAIR, send4.at[there], recv4.at[mine], (me, there)).start()
 
     channel = lax.broadcasted_iota(jnp.int32, (channels, LANES), 0)
     loads[3].wait()
@@ -271,7 +314,9 @@
     def _():
         whole(2 + PAIR, recv4, owners).wait_recv()
 
-    rows4[...] = recv4[...].astype(jnp.float32).reshape(channels * ROWS, LANES)
+    arrived = recv4[...].astype(jnp.float32)
+    rows4[: singles * ROWS, :] = arrived[:singles, :ROWS, :].reshape(singles * ROWS, LANES)
+    rows4[singles * ROWS :, :] = arrived[singles:].reshape((channels - singles) * ROWS, LANES)
     for s in range(ROWS):
         columns = slice(s * LANES, (s + 1) * LANES)
         conv = rows4[pl.ds(s, channels, stride=ROWS), :]
@@ -280,20 +325,27 @@
 
     @pl.when(is_owner)
     def _():
-        whole(0, send1, owners - 1).wait_send()
-        for c in range(PAIR):
-            whole(1 + c, send2.at[c], blocks - 1).wait_send()
+        whole(1, send2.at[0], blocks - 1).wait_send()
         whole(1 + PAIR, send3, blocks - 1).wait_send()
         whole(2 + PAIR, send4, planes - 1).wait_send()
 
+    @pl.when(is_single)
+    def _():
+        whole(0, send1, channels - 1).wait_send()
+
+    @pl.when(is_double)
+    def _():
+        whole(0, send1, channels - PAIR).wait_send()
+        whole(2, send2.at[1], blocks - 1).wait_send()
+
     @pl.when(jnp.logical_not(is_owner))
     def _():
-        whole(0, send1, owners).wait_send()
+        whole(0, send1, channels).wait_send()
 
 
 def local(planes, blocks, outer_gate, inner_gate, signal, filter_taps, skip_gain):
     channels, tokens = signal.shape
-    owners = planes // PAIR
+    owners = sum(layout(planes))
     tables = make_tables(planes, blocks)
     bf16, f32 = jnp.bfloat16, jnp.float32
     scratch = [pltpu.VMEM((channels, tokens), bf16)] * 4
@@ -302,8 +354,8 @@
     scratch += [
         pltpu.VMEM((channels, tokens), f32),
         pltpu.VMEM((channels * 2 * ROWS, LANES), f32),
-        pltpu.VMEM((owners, PAIR * 2 * ROWS, LANES), bf16),
-        pltpu.VMEM((planes, PAIR * 2 * ROWS, LANES), bf16),
+        pltpu.VMEM((channels, 2 * ROWS, LANES), bf16),
+        pltpu.VMEM((planes, PAIR, 2 * ROWS, LANES), bf16),
         pltpu.VMEM((PAIR, blocks, 2 * ROWS, LANES), bf16),
         pltpu.VMEM((PAIR, blocks, 2 * ROWS, LANES), bf16),
     ]

time: 43 us -> 41.7 us (0.970)
  Pallas kernels: 42.2 us -> 40.9 us
    pallas_call x1, Pallas kernels: 42.2 us -> 40.9 us  [local(): pl.pallas_call(functools.partial(kernel, planes, blocks), out_shape=pltpu...]
where the time goes in v4:
time: 41.7 us; the launch traced here: 41.5 us
  Pallas kernels  40.9 us (98%)
  local copies, waits for them, and re-layouts  0.62 us (1%)
    pallas_call x1, Pallas kernels, local(): pl.pallas_call(functools.partial(kernel, planes, blocks), out_shape=pltpu...  40.9 us

profile of v4, /device:TPU:1, one launch (start us, length us, event | category | flops | bytes accessed | tf_op | source)
XLA Modules:
  0.0 41.5 jit_solution(17909839911070284566)
XLA Ops:
  0.0 40.9 %hyena_conv.1 = bf16[16,1024]{1,0:T(8,128)(2,1)S(1)} custom-call(bf16[16,1024]{1,0:T(8,128)(2,1)} %inner_hbm.1, bf16[16,1024]{1,0:T(8,128)(2,1)} %signal_hbm.1, bf16[16,1024]{1,0:T(8,128)(2,1)} %taps_hbm.1, bf16[16,1024]{1,0:T(8,128)(2,1)} %outer_hbm.1, f32[16]{0:T(128)} %skip_hbm.1, bf16[2,512,256]{2,1,0:T(8,128)(2,1)} %constant.12.clone.first_hbm, ...), custom_call_target="tpu_custom_call" | custom-call | tf_op jit(solution)/shard_map/hyena_conv/pallas_call | solution.py:375
  40.9 0.6 %copy.13 = bf16[16,1024]{1,0:T(8,128)(2,1)} copy(bf16[16,1024]{1,0:T(8,128)(2,1)S(1)} %hyena_conv.1) | data formatting | bytes 65536

commit v5 on v4

--- a/solution.py
+++ b/solution.py
@@ -14,7 +14,6 @@
 LANES = 128
 ROWS = 8
 PAIR = 2
-DOUBLES_IN_EIGHT = 3
 
 
 def split_bf16(table):
@@ -91,8 +90,8 @@
 
 
 def layout(planes):
-    doubles = DOUBLES_IN_EIGHT * planes // 8
-    return planes - PAIR * doubles, doubles
+    quarter = planes // 4
+    return quarter, quarter, quarter
 
 
 def kernel(planes, blocks, inner_hbm, signal_hbm, taps_hbm, outer_hbm, skip_hbm, first_hbm, twist_hbm,
@@ -103,18 +102,28 @@
     me = lax.axis_index("ctx")
     plane = lax.axis_index("ch")
     channels = planes
-    singles, doubles = layout(planes)
-    owners = singles + doubles
+    ahead, doubles, behind = layout(planes)
+    owners = ahead + doubles + behind
+
 
     def rank(z):
-        return (z + singles) % planes
+        return (z + ahead) % planes
+
+    def has_two(owner):
+        return jnp.logical_and(owner >= ahead, owner < ahead + doubles)
+
+    def has_one(owner):
+        return jnp.logical_and(owner < owners, jnp.logical_not(has_two(owner)))
+
+    def channel_of(owner):
+        return owner + jnp.clip(owner - ahead, 0, doubles)
 
     units = ROWS * planes
     part = units // blocks
     is_owner = rank(plane) < owners
     mine = rank(plane)
-    is_double = jnp.logical_and(mine >= singles, mine < owners)
-    is_single = mine < singles
+    is_double = has_two(mine)
+    is_single = has_one(mine)
     ring = far_first(planes, True)
     flat = far_first(blocks, False)
 
@@ -158,20 +167,17 @@
             device_id_type=MESH,
         )
 
-    def channel_of(owner):
-        return singles + PAIR * (owner - singles)
-
     def whole(stage, buffer, slots):
         return remote(stage, buffer.at[pl.ds(0, slots)], buffer.at[pl.ds(0, slots)], (me, plane))
 
     for k in ring:
         there = (plane + k) % planes
 
-        @pl.when(rank(there) < singles)
+        @pl.when(has_one(rank(there)))
         def _(there=there):
-            remote(0, send1.at[rank(there)], recv1.at[plane, 0], (me, there)).start()
-
-        @pl.when(jnp.logical_and(rank(there) >= singles, rank(there) < owners))
+            remote(0, send1.at[channel_of(rank(there))], recv1.at[plane, 0], (me, there)).start()
+
+        @pl.when(has_two(rank(there)))
         def _(there=there):
             remote(0, send1.at[pl.ds(channel_of(rank(there)), PAIR)], recv1.at[plane], (me, there)).start()
 
@@ -182,7 +188,7 @@
 
         @pl.when(is_single)
         def _():
-            recv1[plane, 0] = send1[mine]
+            recv1[plane, 0] = send1[channel_of(mine)]
 
         @pl.when(is_double)
         def _():
@@ -315,8 +321,11 @@
         whole(2 + PAIR, recv4, owners).wait_recv()
 
     arrived = recv4[...].astype(jnp.float32)
-    rows4[: singles * ROWS, :] = arrived[:singles, :ROWS, :].reshape(singles * ROWS, LANES)
-    rows4[singles * ROWS :, :] = arrived[singles:].reshape((channels - singles) * ROWS, LANES)
+    row = 0
+    for owner in range(owners):
+        rows = PAIR * ROWS if ahead <= owner < ahead + doubles else ROWS
+        rows4[row : row + rows, :] = arrived[owner, :rows, :]
+        row += rows
     for s in range(ROWS):
         columns = slice(s * LANES, (s + 1) * LANES)
         conv = rows4[pl.ds(s, channels, stride=ROWS), :]

time: 41.7 us -> 40.4 us (0.969)
  Pallas kernels: 40.9 us -> 39.6 us
    pallas_call x1, Pallas kernels: 40.9 us -> 39.6 us  [local(): pl.pallas_call(functools.partial(kernel, planes, blocks), out_shape=pltpu...]
where the time goes in v5:
time: 40.4 us; the launch traced here: 40.2 us
  Pallas kernels  39.6 us (98%)
  local copies, waits for them, and re-layouts  0.62 us (2%)
    pallas_call x1, Pallas kernels, local(): pl.pallas_call(functools.partial(kernel, planes, blocks), out_shape=pltpu...  39.6 us

profile of v5, /device:TPU:1, one launch (start us, length us, event | category | flops | bytes accessed | tf_op | source)
XLA Modules:
  0.0 40.2 jit_solution(2021380469671591365)
XLA Ops:
  0.0 39.6 %hyena_conv.1 = bf16[16,1024]{1,0:T(8,128)(2,1)S(1)} custom-call(bf16[16,1024]{1,0:T(8,128)(2,1)} %inner_hbm.1, bf16[16,1024]{1,0:T(8,128)(2,1)} %signal_hbm.1, bf16[16,1024]{1,0:T(8,128)(2,1)} %taps_hbm.1, bf16[16,1024]{1,0:T(8,128)(2,1)} %outer_hbm.1, f32[16]{0:T(128)} %skip_hbm.1, bf16[2,512,256]{2,1,0:T(8,128)(2,1)} %constant.12.clone.first_hbm, ...), custom_call_target="tpu_custom_call" | custom-call | tf_op jit(solution)/shard_map/hyena_conv/pallas_call | solution.py:384
  39.6 0.6 %copy.13 = bf16[16,1024]{1,0:T(8,128)(2,1)} copy(bf16[16,1024]{1,0:T(8,128)(2,1)S(1)} %hyena_conv.1) | data formatting | bytes 65536

commit v6 on v5

--- a/solution.py
+++ b/solution.py
@@ -94,6 +94,10 @@
     return quarter, quarter, quarter
 
 
+def wrap(position, size):
+    return lax.rem(position, jnp.int32(size))
+
+
 def kernel(planes, blocks, inner_hbm, signal_hbm, taps_hbm, outer_hbm, skip_hbm, first_hbm, twist_hbm,
            second_hbm, back_hbm, untwist_hbm, last_hbm, out_ref,
            inner, signal, taps, outer, skip_scalars, first, twist, second, back, untwist, last,
@@ -107,7 +111,7 @@
 
 
     def rank(z):
-        return (z + ahead) % planes
+        return wrap(z + ahead, planes)
 
     def has_two(owner):
         return jnp.logical_and(owner >= ahead, owner < ahead + doubles)
@@ -129,18 +133,21 @@
 
     barrier = pltpu.get_barrier_semaphore()
 
-    @pl.when(is_owner)
-    def _():
-        for k in ring:
-            pl.semaphore_signal(barrier, inc=1, device_id=(me, (plane + k) % planes), device_id_type=MESH)
-        for k in flat:
-            pl.semaphore_signal(barrier, inc=1, device_id=((me + k) % blocks, plane), device_id_type=MESH)
-
     sources = (inner_hbm, signal_hbm, taps_hbm, outer_hbm, skip_hbm, first_hbm, twist_hbm, second_hbm,
                back_hbm, untwist_hbm, last_hbm)
     places = (inner, signal, taps, outer, skip_scalars, first, twist, second, back, untwist, last)
     loads = [pltpu.make_async_copy(s, d, load_sem.at[i]) for i, (s, d) in enumerate(zip(sources, places))]
-    for load in loads[:5]:
+    for load in loads[:3]:
+        load.start()
+
+    @pl.when(is_owner)
+    def _():
+        for k in ring:
+            pl.semaphore_signal(barrier, inc=1, device_id=(me, wrap(plane + k, planes)), device_id_type=MESH)
+        for k in flat:
+            pl.semaphore_signal(barrier, inc=1, device_id=(wrap(me + k, blocks), plane), device_id_type=MESH)
+
+    for load in loads[3:5]:
         load.start()
     for load in loads[:3]:
         load.wait()
@@ -171,7 +178,7 @@
         return remote(stage, buffer.at[pl.ds(0, slots)], buffer.at[pl.ds(0, slots)], (me, plane))
 
     for k in ring:
-        there = (plane + k) % planes
+        there = wrap(plane + k, planes)
 
         @pl.when(has_one(rank(there)))
         def _(there=there):
@@ -224,7 +231,7 @@
             ).astype(jnp.bfloat16)
             recv2[c, me] = send2[c, me]
             for k in flat:
-                there = (me + k) % blocks
+                there = wrap(me + k, blocks)
                 remote(1 + c, send2.at[c, there], recv2.at[c, me], (there, plane)).start()
 
         forward(0)
@@ -295,15 +302,35 @@
         ).astype(jnp.bfloat16)
         recv4[mine] = send4[plane]
         for k in ring:
-            there = (plane + k) % planes
+            there = wrap(plane + k, planes)
             if 1: continue
             remote(2 + PAIR, send4.at[there], recv4.at[mine], (me, there)).start()
 
-        for there in range(planes):
-
-            @pl.when(there != plane)
-            def _(there=there):
-                remote(2 + PAIR, send4.at[there], recv4.at[mine], (me, there)).start()
+        def deliver(targets, stage):
+            for there in targets:
+
+                @pl.when(there != plane)
+                def _(there=there):
+                    pltpu.make_async_remote_copy(
+                        src_ref=send4.at[there],
+                        dst_ref=recv4.at[mine],
+                        send_sem=send_sem.at[stage],
+                        recv_sem=recv_sem.at[2 + PAIR],
+                        device_id=(me, there),
+                        device_id_type=MESH,
+                    ).start()
+
+            @pl.when(jnp.logical_and(plane >= targets[0], plane <= targets[-1]))
+            def _():
+                whole(stage, send4, len(targets) - 1).wait_send()
+
+            @pl.when(jnp.logical_or(plane < targets[0], plane > targets[-1]))
+            def _():
+                whole(stage, send4, len(targets)).wait_send()
+
+        deliver(range(planes // 4), 2 + PAIR)
+        deliver(range(planes // 4, planes // 2), 3 + PAIR)
+        deliver(range(planes // 2, planes), 4 + PAIR)
 
     channel = lax.broadcasted_iota(jnp.int32, (channels, LANES), 0)
     loads[3].wait()
@@ -336,7 +363,6 @@
     def _():
         whole(1, send2.at[0], blocks - 1).wait_send()
         whole(1 + PAIR, send3, blocks - 1).wait_send()
-        whole(2 + PAIR, send4, planes - 1).wait_send()
 
     @pl.when(is_single)
     def _():
@@ -377,8 +403,8 @@
         pltpu.VMEM((owners, PAIR * ROWS, LANES), bf16),
         pltpu.VMEM((channels * ROWS, LANES), f32),
         pltpu.SemaphoreType.DMA((11,)),
-        pltpu.SemaphoreType.DMA((3 + PAIR,)),
-        pltpu.SemaphoreType.DMA((3 + PAIR,)),
+        pltpu.SemaphoreType.DMA((5 + PAIR,)),
+        pltpu.SemaphoreType.DMA((5 + PAIR,)),
     ]
     operands = (inner_gate, signal, filter_taps, outer_gate, skip_gain, *[jnp.asarray(t) for t in tables])
     return pl.pallas_call(

time: 40.4 us -> 40.4 us (level)
  no operation moved by 1% of the time
where the time goes in v6:
time: 40.4 us; the launch traced here: 40.2 us
  Pallas kernels  39.5 us (98%)
  local copies, waits for them, and re-layouts  0.62 us (2%)
    pallas_call x1, Pallas kernels, local(): pl.pallas_call(functools.partial(kernel, planes, blocks), out_shape=pltpu...  39.5 us

profile of v6, /device:TPU:1, one launch (start us, length us, event | category | flops | bytes accessed | tf_op | source)
XLA Modules:
  0.0 40.2 jit_solution(15575170185889374894)
XLA Ops:
  0.0 39.5 %hyena_conv.1 = bf16[16,1024]{1,0:T(8,128)(2,1)S(1)} custom-call(bf16[16,1024]{1,0:T(8,128)(2,1)} %inner_hbm.1, bf16[16,1024]{1,0:T(8,128)(2,1)} %signal_hbm.1, bf16[16,1024]{1,0:T(8,128)(2,1)} %taps_hbm.1, bf16[16,1024]{1,0:T(8,128)(2,1)} %outer_hbm.1, f32[16]{0:T(128)} %skip_hbm.1, bf16[2,512,256]{2,1,0:T(8,128)(2,1)} %constant.12.clone.first_hbm, ...), custom_call_target="tpu_custom_call" | custom-call | tf_op jit(solution)/shard_map/hyena_conv/pallas_call | solution.py:410
  39.5 0.6 %copy.13 = bf16[16,1024]{1,0:T(8,128)(2,1)} copy(bf16[16,1024]{1,0:T(8,128)(2,1)S(1)} %hyena_conv.1) | data formatting | bytes 65536

commit v7 on v6

--- a/solution.py
+++ b/solution.py
@@ -160,7 +160,7 @@
         columns = slice(s * LANES, (s + 1) * LANES)
         staged[pl.ds(s, channels, stride=2 * ROWS), :] = gated[:, columns]
         staged[pl.ds(ROWS + s, channels, stride=2 * ROWS), :] = filters[:, columns]
-    send1[...] = staged[...].reshape(channels, 2 * ROWS, LANES).astype(jnp.bfloat16)
+    send1[...] = staged[: channels * 2 * ROWS, :].reshape(channels, 2 * ROWS, LANES).astype(jnp.bfloat16)
 
     pl.semaphore_wait(barrier, jnp.where(is_owner, owners + blocks - 2, owners))
 
@@ -388,7 +388,7 @@
     scratch += [pltpu.VMEM(t.shape, t.dtype) for t in tables]
     scratch += [
         pltpu.VMEM((channels, tokens), f32),
-        pltpu.VMEM((channels * 2 * ROWS, LANES), f32),
+        pltpu.VMEM(((channels + 1) * 2 * ROWS, LANES), f32),
         pltpu.VMEM((channels, 2 * ROWS, LANES), bf16),
         pltpu.VMEM((planes, PAIR, 2 * ROWS, LANES), bf16),
         pltpu.VMEM((PAIR, blocks, 2 * ROWS, LANES), bf16),
@@ -401,7 +401,7 @@
         pltpu.VMEM((blocks, PAIR * ROWS, LANES), bf16),
         pltpu.VMEM((planes, PAIR * ROWS, LANES), bf16),
         pltpu.VMEM((owners, PAIR * ROWS, LANES), bf16),
-        pltpu.VMEM((channels * ROWS, LANES), f32),
+        pltpu.VMEM(((channels + 1) * ROWS, LANES), f32),
         pltpu.SemaphoreType.DMA((11,)),
         pltpu.SemaphoreType.DMA((5 + PAIR,)),
         pltpu.SemaphoreType.DMA((5 + PAIR,)),

time: 40.4 us -> 40.4 us (level)
  no operation moved by 1% of the time
where the time goes in v7:
time: 40.4 us; the launch traced here: 40.2 us
  Pallas kernels  39.5 us (98%)
  local copies, waits for them, and re-layouts  0.62 us (2%)
    pallas_call x1, Pallas kernels, local(): pl.pallas_call(functools.partial(kernel, planes, blocks), out_shape=pltpu...  39.5 us

profile of v7, /device:TPU:1, one launch (start us, length us, event | category | flops | bytes accessed | tf_op | source)
XLA Modules:
  0.0 40.2 jit_solution(2940204593330557954)
XLA Ops:
  0.0 39.5 %hyena_conv.1 = bf16[16,1024]{1,0:T(8,128)(2,1)S(1)} custom-call(bf16[16,1024]{1,0:T(8,128)(2,1)} %inner_hbm.1, bf16[16,1024]{1,0:T(8,128)(2,1)} %signal_hbm.1, bf16[16,1024]{1,0:T(8,128)(2,1)} %taps_hbm.1, bf16[16,1024]{1,0:T(8,128)(2,1)} %outer_hbm.1, f32[16]{0:T(128)} %skip_hbm.1, bf16[2,512,256]{2,1,0:T(8,128)(2,1)} %constant.12.clone.first_hbm, ...), custom_call_target="tpu_custom_call" | custom-call | tf_op jit(solution)/shard_map/hyena_conv/pallas_call | solution.py:410
  39.6 0.6 %copy.13 = bf16[16,1024]{1,0:T(8,128)(2,1)} copy(bf16[16,1024]{1,0:T(8,128)(2,1)S(1)} %hyena_conv.1) | data formatting | bytes 65536

commit v8 on v7

--- a/solution.py
+++ b/solution.py
@@ -177,16 +177,19 @@
     def whole(stage, buffer, slots):
         return remote(stage, buffer.at[pl.ds(0, slots)], buffer.at[pl.ds(0, slots)], (me, plane))
 
-    for k in ring:
+    def offer(k, two):
         there = wrap(plane + k, planes)
 
-        @pl.when(has_one(rank(there)))
-        def _(there=there):
-            remote(0, send1.at[channel_of(rank(there))], recv1.at[plane, 0], (me, there)).start()
-
-        @pl.when(has_two(rank(there)))
-        def _(there=there):
-            remote(0, send1.at[pl.ds(channel_of(rank(there)), PAIR)], recv1.at[plane], (me, there)).start()
+        @pl.when(has_two(rank(there)) if two else has_one(rank(there)))
+        def _():
+            if two:
+                remote(0, send1.at[pl.ds(channel_of(rank(there)), PAIR)], recv1.at[plane], (me, there)).start()
+            else:
+                remote(0, send1.at[channel_of(rank(there))], recv1.at[plane, 0], (me, there)).start()
+
+    order = [(k, two) for k in ring for two in (False, True)]
+    for k, two in sorted(order, key=lambda item: -away(item[0], planes, True) - 0.5 * item[1]):
+        offer(k, two)
 
     @pl.when(is_owner)
     def _():
@@ -229,10 +232,10 @@
                 ],
                 axis=1,
             ).astype(jnp.bfloat16)
-            recv2[c, me] = send2[c, me]
             for k in flat:
                 there = wrap(me + k, blocks)
                 remote(1 + c, send2.at[c, there], recv2.at[c, me], (there, plane)).start()
+            recv2[c, me] = send2[c, me]
 
         forward(0)
         pl.when(is_double)(functools.partial(forward, 1))
@@ -273,12 +276,12 @@
             product[:, ROWS:, :] = jnp.zeros((blocks, ROWS, LANES), jnp.float32)
 
         send3[...] = product[...].astype(jnp.bfloat16)
-        recv3[me] = send3[me]
         for there in sorted(range(blocks), key=lambda k: away(k, blocks, False)):
 
             @pl.when(there != me)
             def _(there=there):
                 remote(1 + PAIR, send3.at[there], recv3.at[me], (there, plane)).start()
+        recv3[me] = send3[me]
         whole(1 + PAIR, recv3, blocks - 1).wait_recv()
 
         waves = recv3[...].reshape(blocks * PAIR * ROWS, LANES)

time: 40.4 us -> 40.4 us (level)
  no operation moved by 1% of the time
where the time goes in v8:
time: 40.4 us; the launch traced here: 40.2 us
  Pallas kernels  39.5 us (98%)
  local copies, waits for them, and re-layouts  0.62 us (2%)
    pallas_call x1, Pallas kernels, local(): pl.pallas_call(functools.partial(kernel, planes, blocks), out_shape=pltpu...  39.5 us

profile of v8, /device:TPU:1, one launch (start us, length us, event | category | flops | bytes accessed | tf_op | source)
XLA Modules:
  0.0 40.2 jit_solution(16063269161715455647)
XLA Ops:
  0.0 39.5 %hyena_conv.1 = bf16[16,1024]{1,0:T(8,128)(2,1)S(1)} custom-call(bf16[16,1024]{1,0:T(8,128)(2,1)} %inner_hbm.1, bf16[16,1024]{1,0:T(8,128)(2,1)} %signal_hbm.1, bf16[16,1024]{1,0:T(8,128)(2,1)} %taps_hbm.1, bf16[16,1024]{1,0:T(8,128)(2,1)} %outer_hbm.1, f32[16]{0:T(128)} %skip_hbm.1, bf16[2,512,256]{2,1,0:T(8,128)(2,1)} %constant.12.clone.first_hbm, ...), custom_call_target="tpu_custom_call" | custom-call | tf_op jit(solution)/shard_map/hyena_conv/pallas_call | solution.py:413
  39.5 0.6 %copy.13 = bf16[16,1024]{1,0:T(8,128)(2,1)} copy(bf16[16,1024]{1,0:T(8,128)(2,1)S(1)} %hyena_conv.1) | data formatting | bytes 65536
